TPU v7x, 32 devices: a whole 2x2x4 slice. The times are simulated.
32 devices in a mesh: diamond: 4 (over z), region: 8 (over y, x, core).
Axes of the slice: x: 2, y: 2, z: 4, core: 2. Of those that a mesh axis runs over, the one named last changes fastest.
Arguments:
- height: float32 [8, 256, 512], P(None, 'region', 'diamond'), may hold values from -6 to 6
- wind: float32 [2, 8, 256, 512], P(None, None, 'region', 'diamond'), may hold values from -6 to 6
- cell_area: float32 [256, 512], P('region', 'diamond'), may hold values from 0.5 to 2
- pentagon_flags: int32 [256, 512], P('region', 'diamond'), may hold values 0 or 1
- turn_codes: int32 [4], replicated, may hold values from 0 to 3
Outputs:
- new_height: float32 [8, 256, 512], P(None, 'region', 'diamond')
- new_wind: float32 [2, 8, 256, 512], P(None, None, 'region', 'diamond')
All inputs are finite; a program needn't handle non-finite values. No bound on the sum of `pentagon_flags` on one device may be relied on, other than what follows from the above.
Results may differ from a plain program's by a relative error of at most 0.00002.
Values sent between devices are 32-bit elements; how exact they have to be, the bound alone decides.
A program may use at most 64 MiB of HBM per device.

v0:
```python
import functools

import jax
import jax.numpy as jnp
from jax import lax
from jax.experimental import pallas as pl
from jax.experimental.pallas import tpu as pltpu
from jax.sharding import PartitionSpec as P

STEPS = 3
MESH = pl.DeviceIdType.MESH

time_step = 0.25
damping = 0.02

LEV, ROWS, LANES, PAD = 8, 32, 128, 8
EXT = ROWS + 2 * PAD
HALF = ROWS // 2
STRIP = HALF + 2 * PAD
FIELDS = 5


def shift_lanes(values, amount):
    amount = amount % LANES
    return values if amount == 0 else pltpu.roll(values, amount, values.ndim - 1)


def pieces(total, most):
    sizes = [n for n in range(1, 2 * most) if total % n == 0]
    size = max(n for n in sizes if n <= most)
    if size < most // 2:
        size = max(sizes)
    return total // size, size


def laplace(x, flag):
    count = x.shape[0] - 2
    east = shift_lanes(x[1:], -1)
    west = shift_lanes(x[:-1], 1)
    center = x[1:-1]
    south_west = jnp.where(flag, center, west[:count])
    return (
        ((east[:count] + west[1:]) + (x[2:] + x[:-2]))
        + (east[1:] + south_west)
        - 6.0 * center
    )


def step(state, lap, flux, radius, own_rows, most, basis):
    start = PAD - radius - 2
    count, size = pieces(own_rows + 2 * (radius + 2), most)

    def first(number, carry):
        at = start + number * size
        flag = state[4, pl.ds(at, size)] != 0.0
        for part in range(2):
            lap[part, pl.ds(at, size)] = laplace(state[1 + part, pl.ds(at - 1, size + 2)], flag)
        return carry

    lax.fori_loop(0, count, first, 0)

    start_wind = PAD - radius - 1
    count_wind, size_wind = pieces(own_rows + 2 * (radius + 1), most)

    def second(number, carry):
        at, size = start_wind + number * size_wind, size_wind
        flag = state[4, pl.ds(at, size)] != 0.0
        h = state[0, pl.ds(at - 1, size + 2)]
        center = h[1:-1]
        east = shift_lanes(h[1:], -1)
        west = shift_lanes(h[:-1], 1)
        south_west = jnp.where(flag, center, west[:size])
        diagonal = (east[1:] - south_west) * (0.25 * time_step)
        slope_east = (east[:size] - west[1:]) * (0.5 * time_step) + diagonal
        slope_north = (h[2:] - h[:-2]) * (0.5 * time_step) + diagonal
        if basis is not None:
            cosine, sine = basis
            slope_east, slope_north = (
                slope_east * cosine - slope_north * sine,
                slope_east * sine + slope_north * cosine,
            )
        depth = 1.0 + center
        for part, slope in ((0, slope_east), (1, slope_north)):
            damp = laplace(lap[part, pl.ds(at - 1, size + 2)], flag)
            wind = state[1 + part, pl.ds(at, size)] - (slope + (damping * time_step) * damp)
            state[1 + part, pl.ds(at, size)] = wind
            flux[part, pl.ds(at, size)] = depth * wind
        return carry

    lax.fori_loop(0, count_wind, second, 0)

    start_height = PAD - radius
    count_height, size_height = pieces(own_rows + 2 * radius, most)

    def third(number, carry):
        at, size = start_height + number * size_height, size_height
        flag = state[4, pl.ds(at, size)] != 0.0
        f1 = flux[0, pl.ds(at - 1, size + 2)]
        f2 = flux[1, pl.ds(at - 1, size + 2)]
        if basis is None:
            f3 = f1 + f2
            f3_east = shift_lanes(f3[2:], -1)
            f3_west = jnp.where(flag, f3[1:-1], shift_lanes(f3[:-2], 1))
            c1 = f1[1:-1]
            change = (
                (shift_lanes(c1, -1) - shift_lanes(c1, 1))
                + (f2[2:] - f2[:-2])
                + 0.5 * (f3_east - f3_west)
            )
        else:
            cosine, sine = basis

            def sides(f):
                east = shift_lanes(f[1:], -1)
                west = shift_lanes(f[:-1], 1)
                south_west = jnp.where(flag, f[1:-1], west[:size])
                return east[:size] - west[1:], f[2:] - f[:-2], 0.5 * (east[1:] - south_west)

            ew1, ns1, diag1 = sides(f1)
            ew2, ns2, diag2 = sides(f2)
            change = cosine * ((ew1 + ns2) + (diag1 + diag2)) + sine * (
                (ew2 - ns1) + (diag2 - diag1)
            )
        state[0, pl.ds(at, size)] = state[0, pl.ds(at, size)] - state[3, pl.ds(at, size)] * change
        return carry

    lax.fori_loop(0, count_height, third, 0)


def kernel(
    sizes, turns, height, wind, area, flags, out_height, out_wind,
    h_in, w_in, a_in, p_in, state, lap, flux, strip, strip_lap, strip_flux,
    edge, far, h_out, w_out, local_sem, row_send, row_recv, col_send, col_recv,
):
    diamonds, regions = sizes
    d, r = lax.axis_index("diamond"), lax.axis_index("region")
    left, right = lax.rem(d + diamonds - 1, diamonds), lax.rem(d + 1, diamonds)
    south, north = lax.rem(r + regions - 1, regions), lax.rem(r + 1, regions)

    own = [
        pltpu.make_async_copy(height, h_in.at[:, pl.ds(PAD, ROWS)], local_sem.at[0]),
        pltpu.make_async_copy(wind, w_in.at[:, :, pl.ds(PAD, ROWS)], local_sem.at[1]),
        pltpu.make_async_copy(area, a_in.at[pl.ds(PAD, ROWS)], local_sem.at[2]),
        pltpu.make_async_copy(flags, p_in.at[pl.ds(PAD, ROWS)], local_sem.at[3]),
    ]
    for copy in own:
        copy.start()
    barrier = pltpu.get_barrier_semaphore()
    around = [(x, y) for x in (left, d, right) for y in (south, r, north) if not (x is d and y is r)]
    for place in around:
        pl.semaphore_signal(barrier, inc=1, device_id=place, device_id_type=MESH)
    pl.semaphore_wait(barrier, 8)

    rows = []
    for way, (place, first, to) in enumerate(((south, 0, PAD + ROWS), (north, ROWS - PAD, 0))):
        src, dst = pl.ds(first, PAD), pl.ds(to, PAD)
        for number, (a, b) in enumerate((
            (height.at[:, src], h_in.at[:, dst]),
            (wind.at[:, :, src], w_in.at[:, :, dst]),
            (area.at[src], a_in.at[dst]),
            (flags.at[src], p_in.at[dst]),
        )):
            copy = pltpu.make_async_remote_copy(
                a, b, row_send.at[way, number], row_recv.at[way, number],
                device_id=(d, place), device_id_type=MESH,
            )
            copy.start()
            rows.append(copy)
    for copy in own:
        copy.wait()

    h_flat = h_in.reshape(LEV * EXT, LANES)
    w_flat = w_in.reshape(2 * LEV * EXT, LANES)

    def spread(i):
        state[0, i] = h_flat[pl.ds(i, LEV, stride=EXT), :]
        state[1, i] = w_flat[pl.ds(i, LEV, stride=EXT), :]
        state[2, i] = w_flat[pl.ds(LEV * EXT + i, LEV, stride=EXT), :]
        state[3, i] = jnp.broadcast_to((0.5 * time_step) / a_in[pl.ds(i, 1), :], (LEV, LANES))
        state[4, i] = jnp.broadcast_to(p_in[pl.ds(i, 1), :].astype(jnp.float32), (LEV, LANES))

    for i in range(PAD, PAD + ROWS):
        spread(i)

    lane = lax.broadcasted_iota(jnp.int32, (LEV, LANES), 1)

    def pack(field, carry):
        for half in range(2):
            first = jnp.zeros((LEV, LANES), jnp.float32)
            last = first
            for g in range(16):
                row = (g % 8) + 8 * half + (HALF if g >= 8 else 0)
                turned = shift_lanes(state[field, PAD + row], 8 * g)
                first = jnp.where((lane >= 8 * g) & (lane < 8 * g + 8), turned, first)
                before = (8 * g - 8) % LANES
                last = jnp.where((lane >= before) & (lane < before + 8), turned, last)
            edge[0, half, field] = first
            edge[1, half, field] = last
        return carry

    lax.fori_loop(0, FIELDS, pack, 0)
    columns = []
    for way, place in ((0, left), (1, right)):
        side = 1 - way
        for number, (a, b, region) in enumerate((
            (edge.at[way], far.at[side, pl.ds(0, 2)], r),
            (edge.at[way, 1], far.at[side, 2], north),
            (edge.at[way, 0], far.at[side, 3], south),
        )):
            copy = pltpu.make_async_remote_copy(
                a, b, col_send.at[way, number], col_recv.at[side, number],
                device_id=(place, region), device_id_type=MESH,
            )
            copy.start()
            columns.append(copy)

    for copy in rows:
        copy.wait_recv()
    for i in range(PAD):
        spread(i)
        spread(PAD + ROWS + i)

    in_half = lane % 64
    top = lane < 64
    left_halo, right_halo = in_half < 8, in_half >= 56
    left_group = in_half < 32

    def own_strip(number, carry):
        for field in range(FIELDS):
            low, high = state[field, number], state[field, number + HALF]
            strip[field, number] = jnp.where(
                left_group,
                jnp.where(top, shift_lanes(low, 8), shift_lanes(high, 72)),
                jnp.where(top, shift_lanes(low, 56), shift_lanes(high, 120)),
            )
        return carry

    lax.fori_loop(0, STRIP, own_strip, 0)

    for number in range(STEPS):
        step(state, lap, flux, 2 * (STEPS - 1 - number), ROWS, 12, None)

    def turn(other):
        code = turns[d] - turns[other]
        code = jnp.where(code < 0, code + 4, code)
        return (
            jnp.where(code == 0, 1.0, jnp.where(code == 2, -1.0, 0.0)),
            jnp.where(code == 1, 1.0, jnp.where(code == 3, -1.0, 0.0)),
        )

    left_turn, right_turn = turn(left), turn(right)
    cosine = jnp.where(left_halo, left_turn[0], jnp.where(right_halo, right_turn[0], 1.0))
    sine = jnp.where(left_halo, left_turn[1], jnp.where(right_halo, right_turn[1], 0.0))

    for copy in columns:
        copy.wait_recv()

    first_rows = top
    first_rows_before = (lane < 56) | (lane >= 120)

    def blocks(side, field, mask):
        q1, q2, from_south, from_north = [far[side, n, field] for n in range(4)]
        return (
            shift_lanes(jnp.where(mask, q2, from_south), 64),
            q1,
            q2,
            shift_lanes(jnp.where(mask, from_north, q1), 64),
        )

    for block in range(STRIP // 8):
        near = []
        for field in range(FIELDS):
            near.append((
                blocks(0, field, first_rows_before)[block],
                blocks(1, field, first_rows)[block],
            ))
        for g in range(8):
            at = 8 * block + g
            values = []
            for field in range(FIELDS):
                from_left, from_right = near[field]
                values.append(jnp.where(
                    left_halo,
                    shift_lanes(from_left, 8 - 8 * g),
                    jnp.where(right_halo, shift_lanes(from_right, 56 - 8 * g), strip[field, at]),
                ))
            strip[0, at] = values[0]
            strip[1, at] = values[1] * cosine - values[2] * sine
            strip[2, at] = values[1] * sine + values[2] * cosine
            strip[3, at] = values[3]
            strip[4, at] = values[4]

    for number in range(STEPS):
        step(strip, strip_lap, strip_flux, 2 * (STEPS - 1 - number), HALF, 12, (cosine, sine))

    h_rows = h_out.reshape(LEV * ROWS, LANES)
    w_rows = w_out.reshape(2 * LEV * ROWS, LANES)
    for i in range(HALF):
        for field in range(3):
            both = strip[field, PAD + i]
            for row, to_left, to_right in ((i, -8, 72), (i + HALF, 56, 8)):
                value = jnp.where(
                    lane < 8,
                    shift_lanes(both, to_left),
                    jnp.where(lane >= 120, shift_lanes(both, to_right), state[field, PAD + row]),
                )
                if field == 0:
                    h_rows[pl.ds(row, LEV, stride=ROWS), :] = value
                else:
                    w_rows[pl.ds((field - 1) * LEV * ROWS + row, LEV, stride=ROWS), :] = value
    done = [
        pltpu.make_async_copy(h_out, out_height, local_sem.at[0]),
        pltpu.make_async_copy(w_out, out_wind, local_sem.at[1]),
    ]
    for copy in done:
        copy.start()
    for copy in rows + columns:
        copy.wait_send()
    for copy in done:
        copy.wait()


def body(sizes, height, wind, cell_area, pentagon_flags, turn_codes):
    any_space = pl.BlockSpec(memory_space=pl.ANY)
    f32 = jnp.float32
    return tuple(pl.pallas_call(
        functools.partial(kernel, sizes),
        out_shape=(
            jax.ShapeDtypeStruct(height.shape, f32),
            jax.ShapeDtypeStruct(wind.shape, f32),
        ),
        in_specs=[pl.BlockSpec(memory_space=pltpu.SMEM)] + [any_space] * 4,
        out_specs=(any_space, any_space),
        scratch_shapes=[
            pltpu.VMEM((LEV, EXT, LANES), f32),
            pltpu.VMEM((2, LEV, EXT, LANES), f32),
            pltpu.VMEM((EXT, LANES), f32),
            pltpu.VMEM((EXT, LANES), jnp.int32),
            pltpu.VMEM((FIELDS, EXT, LEV, LANES), f32),
            pltpu.VMEM((2, EXT, LEV, LANES), f32),
            pltpu.VMEM((2, EXT, LEV, LANES), f32),
            pltpu.VMEM((FIELDS, STRIP, LEV, LANES), f32),
            pltpu.VMEM((2, STRIP, LEV, LANES), f32),
            pltpu.VMEM((2, STRIP, LEV, LANES), f32),
            pltpu.VMEM((2, 2, FIELDS, LEV, LANES), f32),
            pltpu.VMEM((2, 4, FIELDS, LEV, LANES), f32),
            pltpu.VMEM((LEV, ROWS, LANES), f32),
            pltpu.VMEM((2, LEV, ROWS, LANES), f32),
            pltpu.SemaphoreType.DMA((4,)),
            pltpu.SemaphoreType.DMA((2, 4)),
            pltpu.SemaphoreType.DMA((2, 4)),
            pltpu.SemaphoreType.DMA((2, 3)),
            pltpu.SemaphoreType.DMA((2, 3)),
        ],
        compiler_params=pltpu.CompilerParams(
            collective_id=0, has_side_effects=True, vmem_limit_bytes=32 * 1024 * 1024
        ),
    )(turn_codes, height, wind, cell_area, pentagon_flags))


def solution(mesh):
    placed = (
        P(None, "region", "diamond"),
        P(None, None, "region", "diamond"),
        P("region", "diamond"),
        P("region", "diamond"),
        P(),
    )
    sizes = (mesh.shape["diamond"], mesh.shape["region"])
    return jax.shard_map(
        functools.partial(body, sizes),
        mesh=mesh,
        in_specs=placed,
        out_specs=(P(None, "region", "diamond"), P(None, None, "region", "diamond")),
        check_vma=False,
    )
```

profile of v0, /device:TPU:0, one launch (start us, length us, event | category | flops | bytes accessed | tf_op | source)
XLA Modules:
  0.0 28.6 jit_solution(16987396884551491647)
XLA Ops:
  0.6 0.0 copy-start
  0.6 0.9 %copy-done = f32[2,8,32,128]{3,2,1,0:T(8,128)S(1)} copy-done((f32[2,8,32,128]{3,2,1,0:T(8,128)S(1)}, f32[2,8,32,128]{3,2,1,0:T(8,128)}, u32[]{:S(2)}) %copy-start) | copy-done | bytes 262168
  1.6 0.0 copy-start.1
  1.6 0.9 %copy-done.1 = f32[8,32,128]{2,1,0:T(8,128)S(1)} copy-done((f32[8,32,128]{2,1,0:T(8,128)S(1)}, f32[8,32,128]{2,1,0:T(8,128)}, u32[]{:S(2)}) %copy-start.1) | copy-done | bytes 131096
  2.5 0.0 copy-start.2
  2.5 0.7 %copy-done.2 = f32[32,128]{1,0:T(8,128)S(1)} copy-done((f32[32,128]{1,0:T(8,128)S(1)}, f32[32,128]{1,0:T(8,128)}, u32[]{:S(2)}) %copy-start.2) | copy-done | bytes 16408
  3.2 0.0 copy-start.3
  3.2 0.7 %copy-done.3 = s32[32,128]{1,0:T(8,128)S(1)} copy-done((s32[32,128]{1,0:T(8,128)S(1)}, s32[32,128]{1,0:T(8,128)}, u32[]{:S(2)}) %copy-start.3) | copy-done | bytes 16408
  3.9 0.0 copy-start.4
  3.9 0.7 %copy-done.4 = s32[4]{0:T(128)S(1)} copy-done((s32[4]{0:T(128)S(1)}, s32[4]{0:T(128)}, u32[]{:S(2)}) %copy-start.4) | copy-done | bytes 40
  4.6 22.7 %shard_map.68 = (f32[8,32,128]{2,1,0:T(8,128)S(1)}, f32[2,8,32,128]{3,2,1,0:T(8,128)S(1)}) custom-call(s32[4]{0:T(128)S(1)} %copy-done.4, f32[8,32,128]{2,1,0:T(8,128)S(1)} %copy-done.1, f32[2,8,32,128]{3,2,1,0:T(8,128)S(1)} %copy-done, f32[32,128]{1,0:T(8,128)S(1)} %copy-done.2, s32[32,128]{1,0:T(8,128)S(1)} %copy-done.3), custom_call_target="tpu_custom_call" | custom-call | tf_op jit(solution)/shard_map/pallas_call | solution.py:326
  27.3 0.7 %copy.9 = f32[8,32,128]{2,1,0:T(8,128)} copy(f32[8,32,128]{2,1,0:T(8,128)S(1)} %get-tuple-element.4) | data formatting | bytes 262144
  27.9 0.7 %copy.10 = f32[2,8,32,128]{3,2,1,0:T(8,128)} copy(f32[2,8,32,128]{3,2,1,0:T(8,128)S(1)} %get-tuple-element.5) | data formatting | bytes 524288
Async XLA Ops:
  0.6 1.0 %copy-start = (f32[2,8,32,128]{3,2,1,0:T(8,128)S(1)}, f32[2,8,32,128]{3,2,1,0:T(8,128)}, u32[]{:S(2)}) copy-start(f32[2,8,32,128]{3,2,1,0:T(8,128)} %wind.1) | copy-start | bytes 786436
  1.6 0.9 %copy-start.1 = (f32[8,32,128]{2,1,0:T(8,128)S(1)}, f32[8,32,128]{2,1,0:T(8,128)}, u32[]{:S(2)}) copy-start(f32[8,32,128]{2,1,0:T(8,128)} %height.1) | copy-start | bytes 393220
  2.5 0.7 %copy-start.2 = (f32[32,128]{1,0:T(8,128)S(1)}, f32[32,128]{1,0:T(8,128)}, u32[]{:S(2)}) copy-start(f32[32,128]{1,0:T(8,128)} %area.1) | copy-start | bytes 49156
  3.2 0.7 %copy-start.3 = (s32[32,128]{1,0:T(8,128)S(1)}, s32[32,128]{1,0:T(8,128)}, u32[]{:S(2)}) copy-start(s32[32,128]{1,0:T(8,128)} %flags.1) | copy-start | bytes 49156
  3.9 0.7 %copy-start.4 = (s32[4]{0:T(128)S(1)}, s32[4]{0:T(128)}, u32[]{:S(2)}) copy-start(s32[4]{0:T(128)} %turns.1) | copy-start | bytes 52
where the time goes:
time: 28.9 us; the launch traced here: 28.6 us
  Pallas kernels  22.7 us (79%)
  local copies, waits for them, and re-layouts  5.3 us (18%)
  between operations  0.65 us (2%)
    pallas_call x1, Pallas kernels, body(): pl.pallas_call(functools.partial(kernel, sizes), out_shape=(jax.ShapeDtyp...  22.7 us
    unnamed x12, local copies, waits for them, and re-layouts  5.3 us

commit v1 on v0

v1 whole, which is shorter than its diff:
```python
import functools

import jax
import jax.numpy as jnp
from jax import lax
from jax.experimental import pallas as pl
from jax.experimental.pallas import tpu as pltpu
from jax.sharding import PartitionSpec as P

STEPS = 3
MESH = pl.DeviceIdType.MESH

time_step = 0.25
damping = 0.02

LEV, ROWS, LANES, PAD = 8, 32, 128, 8
EXT = ROWS + 2 * PAD
HALF = ROWS // 2
STRIP = HALF + 2 * PAD
FIELDS = 5


def shift_lanes(values, amount):
    amount = amount % LANES
    return values if amount == 0 else pltpu.roll(values, amount, values.ndim - 1)


def pieces(total, most):
    sizes = [n for n in range(1, 2 * most) if total % n == 0]
    size = max(n for n in sizes if n <= most)
    if size < most // 2:
        size = max(sizes)
    return total // size, size


def laplace(x, flag):
    count = x.shape[0] - 2
    east = shift_lanes(x[1:], -1)
    west = shift_lanes(x[:-1], 1)
    center = x[1:-1]
    south_west = jnp.where(flag, center, west[:count])
    return (
        ((east[:count] + west[1:]) + (x[2:] + x[:-2]))
        + (east[1:] + south_west)
        - 6.0 * center
    )


def each(count, run):
    def once(number, carry):
        run(number)
        return carry

    lax.fori_loop(0, count, once, 0, unroll=True)


def first_laplace(buffers, at, size, basis):
    state, lap, flux = buffers
    flag = state[4, pl.ds(at, size)] != 0.0
    for part in range(2):
        lap[part, pl.ds(at, size)] = laplace(state[1 + part, pl.ds(at - 1, size + 2)], flag)


def next_wind(buffers, at, size, basis):
    state, lap, flux = buffers
    flag = state[4, pl.ds(at, size)] != 0.0
    h = state[0, pl.ds(at - 1, size + 2)]
    center = h[1:-1]
    east = shift_lanes(h[1:], -1)
    west = shift_lanes(h[:-1], 1)
    south_west = jnp.where(flag, center, west[:size])
    diagonal = (east[1:] - south_west) * (0.25 * time_step)
    slope_east = (east[:size] - west[1:]) * (0.5 * time_step) + diagonal
    slope_north = (h[2:] - h[:-2]) * (0.5 * time_step) + diagonal
    if basis is not None:
        cosine, sine = basis
        slope_east, slope_north = (
            slope_east * cosine - slope_north * sine,
            slope_east * sine + slope_north * cosine,
        )
    depth = 1.0 + center
    for part, slope in ((0, slope_east), (1, slope_north)):
        damp = laplace(lap[part, pl.ds(at - 1, size + 2)], flag)
        wind = state[1 + part, pl.ds(at, size)] - (slope + (damping * time_step) * damp)
        state[1 + part, pl.ds(at, size)] = wind
        flux[part, pl.ds(at, size)] = depth * wind


def next_height(buffers, at, size, basis):
    state, lap, flux = buffers
    flag = state[4, pl.ds(at, size)] != 0.0
    f1 = flux[0, pl.ds(at - 1, size + 2)]
    f2 = flux[1, pl.ds(at - 1, size + 2)]
    if basis is None:
        f3 = f1 + f2
        f3_east = shift_lanes(f3[2:], -1)
        f3_west = jnp.where(flag, f3[1:-1], shift_lanes(f3[:-2], 1))
        c1 = f1[1:-1]
        change = (
            (shift_lanes(c1, -1) - shift_lanes(c1, 1))
            + (f2[2:] - f2[:-2])
            + 0.5 * (f3_east - f3_west)
        )
    else:
        cosine, sine = basis

        def sides(f):
            east = shift_lanes(f[1:], -1)
            west = shift_lanes(f[:-1], 1)
            south_west = jnp.where(flag, f[1:-1], west[:size])
            return east[:size] - west[1:], f[2:] - f[:-2], 0.5 * (east[1:] - south_west)

        ew1, ns1, diag1 = sides(f1)
        ew2, ns2, diag2 = sides(f2)
        change = cosine * ((ew1 + ns2) + (diag1 + diag2)) + sine * (
            (ew2 - ns1) + (diag2 - diag1)
        )
    state[0, pl.ds(at, size)] = state[0, pl.ds(at, size)] - state[3, pl.ds(at, size)] * change


STAGES = (first_laplace, next_wind, next_height)


def inner(buffers, own_rows, most, basis):
    for stage in range(3 * STEPS):
        number, kind = divmod(stage, 3)
        skip = 2 * number + 1 + kind
        count, size = pieces(own_rows - 2 * skip, most)
        each(count, lambda n: STAGES[kind](buffers, PAD + skip + n * size, size, basis))


def outer(buffers, own_rows, basis):
    for stage in range(3 * STEPS):
        number, kind = divmod(stage, 3)
        skip = 2 * number + 1 + kind
        beyond = 2 * (STEPS - number) - kind
        far_start = PAD + own_rows - skip
        near_start = PAD - beyond
        each(2, lambda n: STAGES[kind](
            buffers, near_start + n * (far_start - near_start), skip + beyond, basis))


def kernel(
    sizes, turn_codes, height, wind, area, flags, h_out, w_out, turns,
    h_in, w_in, a_in, p_in, state, lap, flux, strip, strip_lap, strip_flux,
    edge, far, local_sem, row_send, row_recv, col_send, col_recv,
):
    diamonds, regions = sizes
    d, r = lax.axis_index("diamond"), lax.axis_index("region")
    left, right = lax.rem(d + diamonds - 1, diamonds), lax.rem(d + 1, diamonds)
    south, north = lax.rem(r + regions - 1, regions), lax.rem(r + 1, regions)

    own = [
        pltpu.make_async_copy(height, h_in.at[:, pl.ds(PAD, ROWS)], local_sem.at[0]),
        pltpu.make_async_copy(wind, w_in.at[:, :, pl.ds(PAD, ROWS)], local_sem.at[1]),
        pltpu.make_async_copy(area, a_in.at[pl.ds(PAD, ROWS)], local_sem.at[2]),
        pltpu.make_async_copy(flags, p_in.at[pl.ds(PAD, ROWS)], local_sem.at[3]),
        pltpu.make_async_copy(turn_codes, turns, local_sem.at[4]),
    ]
    for copy in own:
        copy.start()
    barrier = pltpu.get_barrier_semaphore()
    around = [(x, y) for x in (left, d, right) for y in (south, r, north) if not (x is d and y is r)]
    for place in around:
        pl.semaphore_signal(barrier, inc=1, device_id=place, device_id_type=MESH)
    pl.semaphore_wait(barrier, 8)

    rows = []
    for way, (place, first, to) in enumerate(((south, 0, PAD + ROWS), (north, ROWS - PAD, 0))):
        src, dst = pl.ds(first, PAD), pl.ds(to, PAD)
        for number, (a, b) in enumerate((
            (height.at[:, src], h_in.at[:, dst]),
            (wind.at[:, :, src], w_in.at[:, :, dst]),
            (area.at[src], a_in.at[dst]),
            (flags.at[src], p_in.at[dst]),
        )):
            copy = pltpu.make_async_remote_copy(
                a, b, row_send.at[way, number], row_recv.at[way, number],
                device_id=(d, place), device_id_type=MESH,
            )
            copy.start()
            rows.append(copy)
    for copy in own:
        copy.wait()

    h_flat = h_in.reshape(LEV * EXT, LANES)
    w_flat = w_in.reshape(2 * LEV * EXT, LANES)

    def given(field, i):
        if field == 0:
            return h_flat[pl.ds(i, LEV, stride=EXT), :]
        if field < 3:
            return w_flat[pl.ds((field - 1) * LEV * EXT + i, LEV, stride=EXT), :]
        return state[field, i]

    def spread(i):
        for field in range(3):
            state[field, i] = given(field, i)
        state[3, i] = jnp.broadcast_to((0.5 * time_step) / a_in[pl.ds(i, 1), :], (LEV, LANES))
        state[4, i] = jnp.broadcast_to(p_in[pl.ds(i, 1), :].astype(jnp.float32), (LEV, LANES))

    for i in range(PAD, PAD + ROWS):
        spread(i)

    lane = lax.broadcasted_iota(jnp.int32, (LEV, LANES), 1)

    def pack(field, carry):
        for half in range(2):
            first = jnp.zeros((LEV, LANES), jnp.float32)
            last = first
            for g in range(16):
                row = (g % 8) + 8 * half + (HALF if g >= 8 else 0)
                turned = shift_lanes(state[field, PAD + row], 8 * g)
                first = jnp.where((lane >= 8 * g) & (lane < 8 * g + 8), turned, first)
                before = (8 * g - 8) % LANES
                last = jnp.where((lane >= before) & (lane < before + 8), turned, last)
            edge[0, half, field] = first
            edge[1, half, field] = last
        return carry

    lax.fori_loop(0, FIELDS, pack, 0)
    columns = []
    for way, place in ((0, left), (1, right)):
        side = 1 - way
        for number, (a, b, region) in enumerate((
            (edge.at[way], far.at[side, pl.ds(0, 2)], r),
            (edge.at[way, 1], far.at[side, 2], north),
            (edge.at[way, 0], far.at[side, 3], south),
        )):
            copy = pltpu.make_async_remote_copy(
                a, b, col_send.at[way, number], col_recv.at[side, number],
                device_id=(place, region), device_id_type=MESH,
            )
            copy.start()
            columns.append((number, copy))

    main = (state, lap, flux)
    inner(main, ROWS, 10, None)

    in_half = lane % 64
    top = lane < 64
    left_halo, right_halo = in_half < 8, in_half >= 56
    left_group = in_half < 32
    top_before = (lane < 56) | (lane >= 120)

    def turn(other):
        code = turns[d] - turns[other]
        code = jnp.where(code < 0, code + 4, code)
        return (
            jnp.where(code == 0, 1.0, jnp.where(code == 2, -1.0, 0.0)),
            jnp.where(code == 1, 1.0, jnp.where(code == 3, -1.0, 0.0)),
        )

    left_turn, right_turn = turn(left), turn(right)
    cosine = jnp.where(left_halo, left_turn[0], jnp.where(right_halo, right_turn[0], 1.0))
    sine = jnp.where(left_halo, left_turn[1], jnp.where(right_halo, right_turn[1], 0.0))
    basis = (cosine, sine)

    def received(block, side, field, mask):
        if block == 0:
            both = jnp.where(mask, far[side, 1, field], far[side, 2, field])
            return shift_lanes(both, 64)
        if block == 3:
            both = jnp.where(mask, far[side, 3, field], far[side, 0, field])
            return shift_lanes(both, 64)
        return far[side, block - 1, field]

    def build(block):
        def one(field):
            from_left = received(block, 0, field, top_before)
            from_right = received(block, 1, field, top)
            for g in range(8):
                at = 8 * block + g
                low, high = given(field, at), given(field, at + HALF)
                mine = jnp.where(
                    left_group,
                    jnp.where(top, shift_lanes(low, 8), shift_lanes(high, 72)),
                    jnp.where(top, shift_lanes(low, 56), shift_lanes(high, 120)),
                )
                strip[field, at] = jnp.where(
                    left_halo,
                    shift_lanes(from_left, 8 - 8 * g),
                    jnp.where(right_halo, shift_lanes(from_right, 56 - 8 * g), mine),
                )

        for field in range(FIELDS):
            one(field)
        where = pl.ds(8 * block, 8)
        east, north = strip[1, where], strip[2, where]
        strip[1, where] = east * cosine - north * sine
        strip[2, where] = east * sine + north * cosine

    edges = (strip, strip_lap, strip_flux)
    for copy in columns:
        if copy[0] == 0:
            copy[1].wait_recv()
    build(1)
    build(2)
    inner(edges, HALF, 10, basis)

    for copy in rows:
        copy.wait_recv()
    for i in range(PAD):
        spread(i)
        spread(PAD + ROWS + i)
    for copy in columns:
        if copy[0] != 0:
            copy[1].wait_recv()
    build(0)
    build(3)
    outer(main, ROWS, None)
    outer(edges, HALF, basis)

    h_rows = h_out.reshape(LEV * ROWS, LANES)
    w_rows = w_out.reshape(2 * LEV * ROWS, LANES)
    for i in range(HALF):
        for field in range(3):
            both = strip[field, PAD + i]
            for row, to_left, to_right in ((i, -8, 72), (i + HALF, 56, 8)):
                value = jnp.where(
                    lane < 8,
                    shift_lanes(both, to_left),
                    jnp.where(lane >= 120, shift_lanes(both, to_right), state[field, PAD + row]),
                )
                if field == 0:
                    h_rows[pl.ds(row, LEV, stride=ROWS), :] = value
                else:
                    w_rows[pl.ds((field - 1) * LEV * ROWS + row, LEV, stride=ROWS), :] = value
    for copy in rows + [copy for _, copy in columns]:
        copy.wait_send()


def body(sizes, height, wind, cell_area, pentagon_flags, turn_codes):
    hbm = pl.BlockSpec(memory_space=pltpu.HBM)
    vmem = pl.BlockSpec(memory_space=pltpu.VMEM)
    f32 = jnp.float32
    return tuple(pl.pallas_call(
        functools.partial(kernel, sizes),
        out_shape=(
            jax.ShapeDtypeStruct(height.shape, f32),
            jax.ShapeDtypeStruct(wind.shape, f32),
        ),
        in_specs=[hbm] * 5,
        out_specs=(vmem, vmem),
        scratch_shapes=[
            pltpu.SMEM(turn_codes.shape, jnp.int32),
            pltpu.VMEM((LEV, EXT, LANES), f32),
            pltpu.VMEM((2, LEV, EXT, LANES), f32),
            pltpu.VMEM((EXT, LANES), f32),
            pltpu.VMEM((EXT, LANES), jnp.int32),
            pltpu.VMEM((FIELDS, EXT, LEV, LANES), f32),
            pltpu.VMEM((2, EXT, LEV, LANES), f32),
            pltpu.VMEM((2, EXT, LEV, LANES), f32),
            pltpu.VMEM((FIELDS, STRIP, LEV, LANES), f32),
            pltpu.VMEM((2, STRIP, LEV, LANES), f32),
            pltpu.VMEM((2, STRIP, LEV, LANES), f32),
            pltpu.VMEM((2, 2, FIELDS, LEV, LANES), f32),
            pltpu.VMEM((2, 4, FIELDS, LEV, LANES), f32),
            pltpu.SemaphoreType.DMA((5,)),
            pltpu.SemaphoreType.DMA((2, 4)),
            pltpu.SemaphoreType.DMA((2, 4)),
            pltpu.SemaphoreType.DMA((2, 3)),
            pltpu.SemaphoreType.DMA((2, 3)),
        ],
        compiler_params=pltpu.CompilerParams(
            collective_id=0, has_side_effects=True, vmem_limit_bytes=32 * 1024 * 1024
        ),
    )(*[
        pltpu.with_memory_space_constraint(x, pltpu.HBM)
        for x in (turn_codes, height, wind, cell_area, pentagon_flags)
    ]))


def solution(mesh):
    placed = (
        P(None, "region", "diamond"),
        P(None, None, "region", "diamond"),
        P("region", "diamond"),
        P("region", "diamond"),
        P(),
    )
    sizes = (mesh.shape["diamond"], mesh.shape["region"])
    return jax.shard_map(
        functools.partial(body, sizes),
        mesh=mesh,
        in_specs=placed,
        out_specs=(P(None, "region", "diamond"), P(None, None, "region", "diamond")),
        check_vma=False,
    )
```

time: 28.9 us -> 18 us (0.62)
  Pallas kernels: 22.7 us -> 15.9 us
  local copies, waits for them, and re-layouts: 5.3 us -> 1.36 us
    pallas_call x1, Pallas kernels: 22.7 us -> 15.9 us  [body(): pl.pallas_call(functools.partial(kernel, sizes), out_shape=(jax.ShapeDtyp...]
    unnamed x12 -> x2, local copies, waits for them, and re-layouts: 5.3 us -> 1.36 us
where the time goes in v1:
time: 18 us; the launch traced here: 17.9 us
  Pallas kernels  15.9 us (88%)
  local copies, waits for them, and re-layouts  1.36 us (8%)
  between operations  0.64 us (4%)
    pallas_call x1, Pallas kernels, body(): pl.pallas_call(functools.partial(kernel, sizes), out_shape=(jax.ShapeDtyp...  15.9 us
    unnamed x2, local copies, waits for them, and re-layouts  1.36 us

profile of v1, /device:TPU:0, one launch (start us, length us, event | category | flops | bytes accessed | tf_op | source)
XLA Modules:
  0.0 17.9 jit_solution(658412335788469161)
XLA Ops:
  0.6 15.9 %shard_map.68 = (f32[8,32,128]{2,1,0:T(8,128)S(1)}, f32[2,8,32,128]{3,2,1,0:T(8,128)S(1)}) custom-call(s32[4]{0:T(128)} %turn_codes.1, f32[8,32,128]{2,1,0:T(8,128)} %height.1, f32[2,8,32,128]{3,2,1,0:T(8,128)} %wind.1, f32[32,128]{1,0:T(8,128)} %area.1, s32[32,128]{1,0:T(8,128)} %flags.1), custom_call_target="tpu_custom_call" | custom-call | tf_op jit(solution)/shard_map/pallas_call | solution.py:337
  16.5 0.7 %copy.9 = f32[8,32,128]{2,1,0:T(8,128)} copy(f32[8,32,128]{2,1,0:T(8,128)S(1)} %get-tuple-element.4) | data formatting | bytes 262144
  17.2 0.7 %copy.10 = f32[2,8,32,128]{3,2,1,0:T(8,128)} copy(f32[2,8,32,128]{3,2,1,0:T(8,128)S(1)} %get-tuple-element.5) | data formatting | bytes 524288

commit v2 on v1

--- a/solution.py
+++ b/solution.py
@@ -18,6 +18,7 @@
 HALF = ROWS // 2
 STRIP = HALF + 2 * PAD
 FIELDS = 5
+SENT = 4
 
 
 def shift_lanes(values, amount):
@@ -129,21 +130,20 @@
         each(count, lambda n: STAGES[kind](buffers, PAD + skip + n * size, size, basis))
 
 
-def outer(buffers, own_rows, basis):
+def outer(parts):
     for stage in range(3 * STEPS):
         number, kind = divmod(stage, 3)
         skip = 2 * number + 1 + kind
         beyond = 2 * (STEPS - number) - kind
-        far_start = PAD + own_rows - skip
-        near_start = PAD - beyond
-        each(2, lambda n: STAGES[kind](
-            buffers, near_start + n * (far_start - near_start), skip + beyond, basis))
+        for buffers, own_rows, basis in parts:
+            for at in (PAD - beyond, PAD + own_rows - skip):
+                STAGES[kind](buffers, at, skip + beyond, basis)
 
 
 def kernel(
     sizes, turn_codes, height, wind, area, flags, h_out, w_out, turns,
     h_in, w_in, a_in, p_in, state, lap, flux, strip, strip_lap, strip_flux,
-    edge, far, local_sem, row_send, row_recv, col_send, col_recv,
+    edge, corner, far, far_corner, local_sem, row_send, row_recv, col_send, col_recv,
 ):
     diamonds, regions = sizes
     d, r = lax.axis_index("diamond"), lax.axis_index("region")
@@ -204,28 +204,37 @@
 
     lane = lax.broadcasted_iota(jnp.int32, (LEV, LANES), 1)
 
-    def pack(field, carry):
+    level = lax.broadcasted_iota(jnp.int32, (LEV, LANES), 0)
+    top = lane < 64
+    top_before = (lane < 56) | (lane >= 120)
+
+    for field in range(SENT):
         for half in range(2):
             first = jnp.zeros((LEV, LANES), jnp.float32)
             last = first
             for g in range(16):
-                row = (g % 8) + 8 * half + (HALF if g >= 8 else 0)
-                turned = shift_lanes(state[field, PAD + row], 8 * g)
+                row = PAD + (g % 8) + 8 * half + (HALF if g >= 8 else 0)
+                value = state[field, row]
+                if field == 3:
+                    value = jnp.where(level < 4, value, state[4, row])
+                turned = shift_lanes(value, 8 * g)
                 first = jnp.where((lane >= 8 * g) & (lane < 8 * g + 8), turned, first)
                 before = (8 * g - 8) % LANES
                 last = jnp.where((lane >= before) & (lane < before + 8), turned, last)
             edge[0, half, field] = first
             edge[1, half, field] = last
-        return carry
-
-    lax.fori_loop(0, FIELDS, pack, 0)
+    for way, mask in ((0, top), (1, top_before)):
+        for pair in range(SENT // 2):
+            even, odd = 2 * pair, 2 * pair + 1
+            corner[way, 0, pair] = jnp.where(mask, shift_lanes(edge[way, 1, even], 64), edge[way, 1, odd])
+            corner[way, 1, pair] = jnp.where(mask, edge[way, 0, even], shift_lanes(edge[way, 0, odd], 64))
     columns = []
     for way, place in ((0, left), (1, right)):
         side = 1 - way
         for number, (a, b, region) in enumerate((
-            (edge.at[way], far.at[side, pl.ds(0, 2)], r),
-            (edge.at[way, 1], far.at[side, 2], north),
-            (edge.at[way, 0], far.at[side, 3], south),
+            (edge.at[way], far.at[side], r),
+            (corner.at[way, 0], far_corner.at[side, 0], north),
+            (corner.at[way, 1], far_corner.at[side, 1], south),
         )):
             copy = pltpu.make_async_remote_copy(
                 a, b, col_send.at[way, number], col_recv.at[side, number],
@@ -238,10 +247,8 @@
     inner(main, ROWS, 10, None)
 
     in_half = lane % 64
-    top = lane < 64
     left_halo, right_halo = in_half < 8, in_half >= 56
     left_group = in_half < 32
-    top_before = (lane < 56) | (lane >= 120)
 
     def turn(other):
         code = turns[d] - turns[other]
@@ -256,14 +263,25 @@
     sine = jnp.where(left_halo, left_turn[1], jnp.where(right_halo, right_turn[1], 0.0))
     basis = (cosine, sine)
 
+    def received_sent(block, side, field, mask):
+        odd = field % 2 == 1
+        if block == 0:
+            same, other = far[side, 1, field], far_corner[side, 0, field // 2]
+            if odd:
+                return shift_lanes(jnp.where(mask, same, other), 64)
+            return jnp.where(mask, other, shift_lanes(same, 64))
+        if block == 3:
+            same, other = far[side, 0, field], far_corner[side, 1, field // 2]
+            if odd:
+                return jnp.where(mask, shift_lanes(same, 64), other)
+            return shift_lanes(jnp.where(mask, other, same), 64)
+        return far[side, block - 1, field]
+
     def received(block, side, field, mask):
-        if block == 0:
-            both = jnp.where(mask, far[side, 1, field], far[side, 2, field])
-            return shift_lanes(both, 64)
-        if block == 3:
-            both = jnp.where(mask, far[side, 3, field], far[side, 0, field])
-            return shift_lanes(both, 64)
-        return far[side, block - 1, field]
+        if field < 3:
+            return received_sent(block, side, field, mask)
+        both = received_sent(block, side, 3, mask)
+        return jnp.broadcast_to(both[4 * field - 12:4 * field - 11], (LEV, LANES))
 
     def build(block):
         def one(field):
@@ -308,8 +326,7 @@
             copy[1].wait_recv()
     build(0)
     build(3)
-    outer(main, ROWS, None)
-    outer(edges, HALF, basis)
+    outer(((main, ROWS, None), (edges, HALF, basis)))
 
     h_rows = h_out.reshape(LEV * ROWS, LANES)
     w_rows = w_out.reshape(2 * LEV * ROWS, LANES)
@@ -330,11 +347,23 @@
         copy.wait_send()
 
 
+def place(height, wind, out_height, out_wind, sems):
+    copies = [
+        pltpu.make_async_copy(height, out_height, sems.at[0]),
+        pltpu.make_async_copy(wind.at[0], out_wind.at[0], sems.at[1]),
+        pltpu.make_async_copy(wind.at[1], out_wind.at[1], sems.at[2]),
+    ]
+    for copy in copies:
+        copy.start()
+    for copy in copies:
+        copy.wait()
+
+
 def body(sizes, height, wind, cell_area, pentagon_flags, turn_codes):
     hbm = pl.BlockSpec(memory_space=pltpu.HBM)
     vmem = pl.BlockSpec(memory_space=pltpu.VMEM)
     f32 = jnp.float32
-    return tuple(pl.pallas_call(
+    results = pl.pallas_call(
         functools.partial(kernel, sizes),
         out_shape=(
             jax.ShapeDtypeStruct(height.shape, f32),
@@ -354,8 +383,10 @@
             pltpu.VMEM((FIELDS, STRIP, LEV, LANES), f32),
             pltpu.VMEM((2, STRIP, LEV, LANES), f32),
             pltpu.VMEM((2, STRIP, LEV, LANES), f32),
-            pltpu.VMEM((2, 2, FIELDS, LEV, LANES), f32),
-            pltpu.VMEM((2, 4, FIELDS, LEV, LANES), f32),
+            pltpu.VMEM((2, 2, SENT, LEV, LANES), f32),
+            pltpu.VMEM((2, 2, SENT // 2, LEV, LANES), f32),
+            pltpu.VMEM((2, 2, SENT, LEV, LANES), f32),
+            pltpu.VMEM((2, 2, SENT // 2, LEV, LANES), f32),
             pltpu.SemaphoreType.DMA((5,)),
             pltpu.SemaphoreType.DMA((2, 4)),
             pltpu.SemaphoreType.DMA((2, 4)),
@@ -368,7 +399,19 @@
     )(*[
         pltpu.with_memory_space_constraint(x, pltpu.HBM)
         for x in (turn_codes, height, wind, cell_area, pentagon_flags)
-    ]))
+    ])
+    whole = pl.BlockSpec(memory_space=pl.ANY)
+    return tuple(pl.pallas_call(
+        place,
+        out_shape=(
+            jax.ShapeDtypeStruct(height.shape, f32),
+            jax.ShapeDtypeStruct(wind.shape, f32),
+        ),
+        in_specs=[whole, whole],
+        out_specs=(whole, whole),
+        scratch_shapes=[pltpu.SemaphoreType.DMA((3,))],
+        compiler_params=pltpu.CompilerParams(vmem_limit_bytes=1024 * 1024),
+    )(*results))
 
 
 def solution(mesh):

time: 18 us -> 17 us (0.944)
  local copies, waits for them, and re-layouts: 1.36 us -> 0 us
  Pallas kernels: 15.9 us -> 16.2 us
    unnamed x2 -> x0, local copies, waits for them, and re-layouts: 1.36 us -> none
    pallas_call x0 -> x1, Pallas kernels: none -> 0.77 us  [body(): pl.pallas_call(place, out_shape=(jax.ShapeDtypeStruct(height.shape, f32),...]
    pallas_call x1, Pallas kernels: 15.9 us -> 15.4 us  [body(): pl.pallas_call(functools.partial(kernel, sizes), out_shape=(jax.ShapeDtyp...]
where the time goes in v2:
time: 17 us; the launch traced here: 16.8 us
  Pallas kernels  16.2 us (95%)
  between operations  0.64 us (4%)
    pallas_call x1, Pallas kernels, body(): pl.pallas_call(functools.partial(kernel, sizes), out_shape=(jax.ShapeDtyp...  15.4 us
    pallas_call x1, Pallas kernels, body(): pl.pallas_call(place, out_shape=(jax.ShapeDtypeStruct(height.shape, f32),...  0.77 us

profile of v2, /device:TPU:0, one launch (start us, length us, event | category | flops | bytes accessed | tf_op | source)
XLA Modules:
  0.0 16.8 jit_solution(10233488236216110630)
XLA Ops:
  0.6 15.4 %shard_map.68 = (f32[8,32,128]{2,1,0:T(8,128)S(1)}, f32[2,8,32,128]{3,2,1,0:T(8,128)S(1)}) custom-call(s32[4]{0:T(128)} %turn_codes.1, f32[8,32,128]{2,1,0:T(8,128)} %height.1, f32[2,8,32,128]{3,2,1,0:T(8,128)} %wind.1, f32[32,128]{1,0:T(8,128)} %area.1, s32[32,128]{1,0:T(8,128)} %flags.1), custom_call_target="tpu_custom_call" | custom-call | tf_op jit(solution)/shard_map/pallas_call | solution.py:366
  16.1 0.8 %shard_map.69 = (f32[8,32,128]{2,1,0:T(8,128)}, f32[2,8,32,128]{3,2,1,0:T(8,128)}) custom-call(f32[8,32,128]{2,1,0:T(8,128)S(1)} %get-tuple-element.4.height, f32[2,8,32,128]{3,2,1,0:T(8,128)S(1)} %get-tuple-element.5.wind), custom_call_target="tpu_custom_call" | custom-call | tf_op jit(solution)/shard_map/pallas_call | solution.py:404
